TPU v7x, 32 devices: a whole 2x2x4 slice. The times are simulated.
32 devices in a mesh: tm: 4 (over y, x), rows: 8 (over z, core).
Axes of the slice: x: 2, y: 2, z: 4, core: 2. Of those that a mesh axis runs over, the one named last changes fastest.
Arguments:
- latents: bfloat16 [64, 16, 10240], P('tm', 'rows')
- video_patch_choice: int32 [2], replicated, may hold values from 0 to 31
- video_patch_degrees: int32 [2], replicated, may hold values from 16 to 64, as said below
- first_norm_gain: float32 [320], replicated, may hold values from 0.5 to 1.5
- first_norm_shift: float32 [320], replicated, may hold values from -3 to 3
- first_conv_weight: bfloat16 [3, 3, 320, 320], replicated, may hold values from -0.109375 to 0.109375
- timestep_bias: float32 [320], replicated, may hold values from -3 to 3
- second_norm_gain: float32 [320], replicated, may hold values from 0.5 to 1.5
- second_norm_shift: float32 [320], replicated, may hold values from -3 to 3
- second_conv_weight: bfloat16 [3, 3, 320, 320], replicated, may hold values from -0.109375 to 0.109375
- second_conv_bias: float32 [320], replicated, may hold values from -3 to 3
- third_norm_gain: float32 [320], replicated, may hold values from 0.5 to 1.5
- third_norm_shift: float32 [320], replicated, may hold values from -3 to 3
- input_projection_weight: bfloat16 [320, 320], replicated, may hold values from -0.3125 to 0.3125
- input_projection_bias: float32 [320], replicated, may hold values from -3 to 3
- layer_norm_gain: float32 [320], replicated, may hold values from 0.5 to 1.5
- layer_norm_shift: float32 [320], replicated, may hold values from -3 to 3
- attention_weight: bfloat16 [4, 320, 320], replicated, may hold values from -0.3125 to 0.3125
- attention_output_bias: float32 [320], replicated, may hold values from -3 to 3
- patch_lowering_store: bfloat16 [32, 4, 320, 64], P(('tm', 'rows')), may hold values from -0.3125 to 0.3125
- patch_raising_store: bfloat16 [32, 4, 64, 320], P(('tm', 'rows')), may hold values from -0.75 to 0.75
- output_projection_weight: bfloat16 [320, 320], replicated, may hold values from -0.3125 to 0.3125
- output_projection_bias: float32 [320], replicated, may hold values from -3 to 3
Outputs:
- block_out: bfloat16 [64, 16, 10240], P('tm', 'rows')
Inputs may be any that keep to these rules, and one draw needn't show every extreme that they name: video_patch_degrees of at least one clip equals 64.
All inputs are finite; a program needn't handle non-finite values.
Results may differ from a plain program's by a relative error of at most 0.019.
Values may be sent and summed in bfloat16 or wider, within the bound.
A program may use at most 128 MiB of HBM per device.

v0:
```python
import math

import jax
import jax.numpy as jnp
from jax import lax
from jax.sharding import PartitionSpec as P

FEATURE_WIDTH = 320
GROUPS = 32
HEADS = 8
PATCH_DEGREE_TOP = 64
W = 32
CLIP_LEN = 32
HD = 40


EPS = 1e-05


def extended_2(shard, sides, width):
    for axis, dim in sides:
        count, length = (lax.axis_size(axis), shard.shape[dim])
        up = [(i, (i + 1) % count) for i in range(count - 1)]
        down = [(j, i) for i, j in up]
        last = lax.slice_in_dim(shard, length - width, length, axis=dim)
        first = lax.slice_in_dim(shard, 0, width, axis=dim)
        before = lax.ppermute(last, axis, up)
        after = lax.ppermute(first, axis, down)
        shard = jnp.concatenate([before, shard, after], axis=dim)
    return shard


def spread(block, axis, source):
    block = jnp.where(lax.axis_index(axis) == source, block, jnp.zeros_like(block))
    return lax.psum(block, axis)


def group_stats(values, count):
    frames, extent = (values.shape[0], values.shape[1])
    parts = values.reshape(frames, extent * W, GROUPS, FEATURE_WIDTH // GROUPS)
    leading_entry = jnp.sum(parts, axis=(1, 3))
    second = jnp.sum(parts * parts, axis=(1, 3))
    total_one, total_two = lax.psum((leading_entry, second), "rows")
    mean = total_one / count
    var = total_two / count - mean * mean
    return (mean, lax.rsqrt(var + EPS))


def apply_norm(values, mean, inv_std, gain, shift):
    frames, extent = (values.shape[0], values.shape[1])
    parts = values.reshape(frames, extent, W, GROUPS, FEATURE_WIDTH // GROUPS)
    normed = (parts - mean[:, None, None, :, None]) * inv_std[:, None, None, :, None]
    return normed.reshape(values.shape) * gain + shift


def conv_valid(extended, kernel):
    frames, extent = (extended.shape[0], extended.shape[1])
    padded = jnp.pad(extended, ((0, 0), (0, 0), (1, 1), (0, 0)))
    stacked = jnp.concatenate(
        [padded[:, :, 0:W], padded[:, :, 1 : W + 1], padded[:, :, 2 : W + 2]], axis=-1
    )
    folded = kernel.reshape(3, 3 * FEATURE_WIDTH, FEATURE_WIDTH)
    total = jnp.zeros((frames * (extent - 2) * W, FEATURE_WIDTH), jnp.float32)
    for shift_row in range(3):
        window = stacked[:, shift_row : shift_row + extent - 2].reshape(-1, 3 * FEATURE_WIDTH)
        total = total + jnp.dot(window, folded[shift_row], preferred_element_type=jnp.float32)
    return total.reshape(frames, extent - 2, W, FEATURE_WIDTH)


def rim_conv(activ, kernel):
    extended = extended_2(activ, (("rows", 1),), 1)
    return conv_valid(extended, kernel)


def positional(times):
    index = jnp.arange(FEATURE_WIDTH, dtype=jnp.int32)
    freq = jnp.exp(-(index // 2 * 2).astype(jnp.float32) * (math.log(10000.0) / FEATURE_WIDTH))
    angle = times[:, None] * freq[None, :]
    return jnp.where(index[None, :] % 2 == 0, jnp.sin(angle), jnp.cos(angle))


def per_device(
    latents,
    video_patch_choice,
    video_patch_degrees,
    first_norm_gain,
    first_norm_shift,
    first_conv_weight,
    timestep_bias,
    second_norm_gain,
    second_norm_shift,
    second_conv_weight,
    second_conv_bias,
    third_norm_gain,
    third_norm_shift,
    input_projection_weight,
    input_projection_bias,
    layer_norm_gain,
    layer_norm_shift,
    attention_weight,
    attention_output_bias,
    patch_lowering_store,
    patch_raising_store,
    output_projection_weight,
    output_projection_bias,
):
    frames, strip = (latents.shape[0], latents.shape[1])
    strips = lax.axis_size("rows")
    count = strip * strips * W * (FEATURE_WIDTH // GROUPS)
    xin = latents.reshape(frames, strip, W, FEATURE_WIDTH)
    xfloat = xin.astype(jnp.float32)
    clip_down_factor = patch_lowering_store[0]
    clip_up_factor = patch_raising_store[0]

    def gather_panel(carry, pair):
        owner, degree_applied = pair
        got_down, got_up = (
            spread(clip_down_factor, ("tm", "rows"), owner),
            spread(clip_up_factor, ("tm", "rows"), owner),
        )
        degree_filter = (jnp.arange(PATCH_DEGREE_TOP, dtype=jnp.int32) < degree_applied).astype(
            jnp.bfloat16
        )
        return (carry, (got_down * degree_filter, got_up))

    ignored_value, (down_factors, up_factors) = lax.scan(
        gather_panel, jnp.zeros((), jnp.int32), (video_patch_choice, video_patch_degrees)
    )
    mean_one, inv_one = group_stats(xfloat, count)
    act1 = jax.nn.silu(
        apply_norm(xfloat, mean_one, inv_one, first_norm_gain, first_norm_shift)
    ).astype(jnp.bfloat16)
    hid1 = (rim_conv(act1, first_conv_weight) + timestep_bias).astype(jnp.bfloat16)
    hid_float = hid1.astype(jnp.float32)
    mean_two, inv_two = group_stats(hid_float, count)
    act2 = jax.nn.silu(
        apply_norm(hid_float, mean_two, inv_two, second_norm_gain, second_norm_shift)
    ).astype(jnp.bfloat16)
    res = (xfloat + rim_conv(act2, second_conv_weight) + second_conv_bias).astype(jnp.bfloat16)
    res_float = res.astype(jnp.float32)
    mean_three, inv_three = group_stats(res_float, count)
    normed = apply_norm(res_float, mean_three, inv_three, third_norm_gain, third_norm_shift).astype(
        jnp.bfloat16
    )
    proj = (
        jnp.dot(
            normed.reshape(-1, FEATURE_WIDTH),
            input_projection_weight,
            preferred_element_type=jnp.float32,
        )
        + input_projection_bias
    ).astype(jnp.bfloat16)
    proj_float = proj.astype(jnp.float32)
    centre = proj_float - jnp.mean(proj_float, axis=-1, keepdims=True)
    layer = (
        centre
        * lax.rsqrt(jnp.mean(centre * centre, axis=-1, keepdims=True) + EPS)
        * layer_norm_gain
        + layer_norm_shift
    )
    frame_index = lax.axis_index("tm") * frames + jnp.arange(frames, dtype=jnp.int32)
    stamps = (frame_index % CLIP_LEN).astype(jnp.float32)
    normal_in = (
        layer.reshape(frames, strip * W, FEATURE_WIDTH) + positional(stamps)[:, None, :]
    ).astype(jnp.bfloat16)
    clip_of = frame_index // CLIP_LEN
    frame_down = down_factors[clip_of]
    frame_up = up_factors[clip_of]

    def clip_adapter(source_bank, projection_index):
        low = jnp.einsum(
            "kfpc,kcr->kfpr",
            source_bank,
            down_factors[:, projection_index],
            preferred_element_type=jnp.float32,
        ).astype(jnp.bfloat16)
        return jnp.einsum(
            "kfpr,krc->kfpc",
            low,
            up_factors[:, projection_index],
            preferred_element_type=jnp.float32,
        )

    scale = 1.0 / math.sqrt(HD)
    factor_slice = lax.all_to_all(
        normal_in.reshape(frames, strip, W * FEATURE_WIDTH),
        "tm",
        split_axis=2,
        concat_axis=0,
        tiled=True,
    )
    total_frames = factor_slice.shape[0]
    rank_limited = factor_slice.reshape(total_frames // CLIP_LEN, CLIP_LEN, -1, FEATURE_WIDTH)

    def remote_project(projection_index):
        base_result = jnp.dot(
            rank_limited.reshape(-1, FEATURE_WIDTH),
            attention_weight[projection_index],
            preferred_element_type=jnp.float32,
        ).reshape(rank_limited.shape)
        return (
            (base_result + clip_adapter(rank_limited, projection_index))
            .astype(jnp.bfloat16)
            .reshape(factor_slice.shape)
        )

    query = remote_project(0)
    total_frames = query.shape[0]
    items = query.shape[1]
    pixels = items * (query.shape[2] // FEATURE_WIDTH)
    clips = total_frames // CLIP_LEN
    heads_shape = (clips, CLIP_LEN, pixels, HEADS, HD)
    scores = (
        jnp.einsum(
            "kfphd,kgphd->kphfg",
            query.reshape(heads_shape),
            remote_project(1).reshape(heads_shape),
            preferred_element_type=jnp.float32,
        )
        * scale
    )
    weights = jax.nn.softmax(scores, axis=-1).astype(jnp.bfloat16)
    attended = jnp.einsum(
        "kphfg,kgphd->kfphd",
        weights,
        remote_project(2).reshape(heads_shape),
        preferred_element_type=jnp.float32,
    ).astype(jnp.bfloat16)
    attended = attended.reshape(total_frames, items, -1)
    attended = lax.all_to_all(attended, "tm", split_axis=0, concat_axis=2, tiled=True)
    att_flat = attended.reshape(frames, strip * W, FEATURE_WIDTH)
    base_out = jnp.dot(
        att_flat.reshape(-1, FEATURE_WIDTH), attention_weight[3], preferred_element_type=jnp.float32
    ).reshape(att_flat.shape)
    low = jnp.einsum(
        "fnc,fcr->fnr", att_flat, frame_down[:, 3], preferred_element_type=jnp.float32
    ).astype(jnp.bfloat16)
    mixed = (
        proj_float.reshape(frames, strip * W, FEATURE_WIDTH)
        + base_out
        + jnp.einsum("fnr,frc->fnc", low, frame_up[:, 3], preferred_element_type=jnp.float32)
        + attention_output_bias
    ).astype(jnp.bfloat16)
    final = (
        res_float.reshape(frames, strip * W, FEATURE_WIDTH)
        + jnp.dot(
            mixed.reshape(-1, FEATURE_WIDTH),
            output_projection_weight,
            preferred_element_type=jnp.float32,
        ).reshape(frames, strip * W, FEATURE_WIDTH)
        + output_projection_bias
    )
    return final.astype(jnp.bfloat16).reshape(frames, strip, W * FEATURE_WIDTH)


def solution(mesh):
    in_specs = (
        P("tm", "rows", None),
        P(),
        P(),
        P(),
        P(),
        P(),
        P(),
        P(),
        P(),
        P(),
        P(),
        P(),
        P(),
        P(),
        P(),
        P(),
        P(),
        P(),
        P(),
        P(("tm", "rows"), None, None, None),
        P(("tm", "rows"), None, None, None),
        P(),
        P(),
    )
    out_specs = P("tm", "rows", None)
    return jax.shard_map(
        per_device, mesh=mesh, in_specs=in_specs, out_specs=out_specs, check_vma=False
    )
```

profile of v0, /device:TPU:0, one launch (start us, length us, event | category | flops | bytes accessed | tf_op | source)
XLA Modules:
  0.0 618.8 jit_solution(351169567533193949)
XLA Ops:
  6.5 21.8 %reshape.332 = f32[16,64,32,10]{3,2,1,0:T(8,128)} reshape(bf16[16,2,10240]{2,1,0:T(2,128)(2,1)} %param.25) | data formatting | bytes 1966080 | tf_op jit(solution)/shard_map/convert_element_type | solution.py:111
  28.4 1.9 reshape.331
  30.3 9.0 %fusion.58 = (f32[16,32]{1,0:T(8,128)S(1)}, f32[16,32]{1,0:T(8,128)S(1)}) fusion(f32[16,64,32,10]{3,2,1,0:T(8,128)} %reshape.332), kind=kLoop, calls=%fused_computation.132 | loop fusion | flops 982016 | bytes 1314816 | tf_op jit(solution)/shard_map/reduce_sum | solution.py:41
  39.3 30.2 %all-reduce.5 = (f32[16,32]{1,0:T(8,128)S(1)}, f32[16,32]{1,0:T(8,128)S(1)}) all-reduce(f32[16,32]{1,0:T(8,128)S(1)} %get-tuple-element.46, f32[16,32]{1,0:T(8,128)S(1)} %get-tuple-element.45), channel_id=1, replica_groups=mesh['tm'=4,'rows'=8] {'rows'}, use_global_device_ids=true, to_apply=%region_3.4 | all-reduce | flops 1024 | bytes 8192 | tf_op jit(solution)/shard_map/psum | solution.py:43
  70.2 1.9 multiply_convert_fusion.1
  73.5 1.5 collective-permute-start.1
  75.2 1.8 fusion.62
  79.2 2.4 pad_maximum_fusion
  85.3 2.2 reshape.320
  87.5 1.6 copy.119
  89.1 2.6 convert_reduce_fusion.1
  91.9 29.9 %all-reduce.4 = (f32[16,32]{1,0:T(8,128)S(1)}, f32[16,32]{1,0:T(8,128)S(1)}) all-reduce(f32[16,32]{1,0:T(8,128)S(1)} %copy.121, f32[16,32]{1,0:T(8,128)S(1)} %copy.120), channel_id=1, replica_groups=mesh['tm'=4,'rows'=8] {'rows'}, use_global_device_ids=true, to_apply=%region_7.8 | all-reduce | flops 1024 | bytes 8192 | tf_op jit(solution)/shard_map/psum | solution.py:43
  122.4 2.0 multiply_convert_fusion
  126.7 1.7 collective-permute-start.3
  128.6 1.9 reshape.333
  130.6 2.9 copy.123
  133.6 2.3 add.310
  137.1 1.8 fusion.61
  138.9 2.0 select_maximum_fusion
  142.0 3.3 pad_maximum_fusion.1
  149.0 2.2 reshape.325
  151.2 10.7 %copy.124 = f32[16,64,32,10]{3,2,1,0:T(8,128)} copy(f32[16,64,32,10]{1,0,3,2:T(8,128)} %reshape.325) | data formatting | bytes 2621440 | tf_op jit(solution)/shard_map/reshape | solution.py:67
  161.9 12.1 %convert_reduce_fusion = (f32[16,32]{1,0:T(8,128)S(1)}, f32[16,32]{1,0:T(8,128)S(1)}) fusion(f32[32,10]{1,0:T(8,128)S(1)} %add.293, f32[16,64,32,10]{3,2,1,0:T(8,128)} %reshape.332, f32[16,64,32,10]{3,2,1,0:T(8,128)} %copy.124), kind=kLoop, calls=%fused_computation.9 | loop fusion | flops 2292736 | bytes 2626816 | tf_op jit(solution)/shard_map/reduce_sum | solution.py:41
  174.0 28.0 %all-reduce.3 = (f32[16,32]{1,0:T(8,128)S(1)}, f32[16,32]{1,0:T(8,128)S(1)}) all-reduce(f32[16,32]{1,0:T(8,128)S(1)} %get-tuple-element.48, f32[16,32]{1,0:T(8,128)S(1)} %get-tuple-element.47), channel_id=1, replica_groups=mesh['tm'=4,'rows'=8] {'rows'}, use_global_device_ids=true, to_apply=%region_11.12 | all-reduce | flops 1024 | bytes 8192 | tf_op jit(solution)/shard_map/psum | solution.py:43
  203.5 2.9 copy.125
  208.1 2.9 copy.126
  211.1 2.9 fusion.67
  216.4 3.0 copy.128
  219.3 3.3 reshape.327
  222.6 2.4 add_convert_fusion.9
  225.0 8.0 %copy.129 = bf16[16,2,10240]{0,1,2:T(2,128)(2,1)} copy(bf16[16,2,10240]{2,1,0:T(2,128)(2,1)S(1)} %add_convert_fusion.9) | data formatting | bytes 1310720 | tf_op jit(solution)/shard_map/convert_element_type | solution.py:165
  233.0 7.5 %reshape.361 = bf16[4,2,40960]{2,1,0:T(2,128)(2,1)} reshape(bf16[10240,2,16]{2,1,0:T(2,128)(2,1)} %bitcast.157) | data formatting | bytes 1310720
  240.5 4.4 all-to-all-start
  244.9 270.4 %while.12 = (s32[]{:T(128)}, bf16[2,4,320,64]{3,2,1,0:T(8,128)(2,1)S(1)}, bf16[2,4,64,320]{3,2,1,0:T(8,128)(2,1)S(1)}, s32[2]{0:T(128)S(1)}, bf16[4,320,64]{2,1,...) while((s32[]{:T(128)}, ...), condition=%wide.region_17.18_spmd, body=%wide.region_14.17_spmd.sunk | while | flops 655498 | bytes 3867544 | solution.py:126
  249.0 128.9 %all-reduce.10.cloned.1.call-done = (bf16[4,320,64]{2,1,0:T(8,128)(2,1)}, bf16[1,4,64,320]{3,2,1,0:T(8,128)(2,1)}) async-done(((bf16[4,320,64]{2,1,0:T(8,128)(2,1)}, bf16[1,4,64,320]{3,2,1,0:T(8,128)(2,1)}), (bf16[4,320,64]{2,1,0:T(8,128)(2,1)}, bf16[1,4,64,320]{3,2,1,0:T(8,128)(2,1)})) %all-reduce.10.cloned.1.call-update) | async-done | bytes 327696 | tf_op jit(solution)/shard_map/while/body/eval_jaxpr/psum | solution.py:35
  384.1 129.2 %all-reduce.10.cloned.1.call-done = (bf16[4,320,64]{2,1,0:T(8,128)(2,1)}, bf16[1,4,64,320]{3,2,1,0:T(8,128)(2,1)}) async-done(((bf16[4,320,64]{2,1,0:T(8,128)(2,1)}, bf16[1,4,64,320]{3,2,1,0:T(8,128)(2,1)}), (bf16[4,320,64]{2,1,0:T(8,128)(2,1)}, bf16[1,4,64,320]{3,2,1,0:T(8,128)(2,1)})) %all-reduce.10.cloned.1.call-update) | async-done | bytes 327696 | tf_op jit(solution)/shard_map/while/body/eval_jaxpr/psum | solution.py:35
  516.4 6.0 reshape.362
  522.4 12.0 %copy.158 = bf16[16,2,4,2560]{3,2,0,1:T(4,128)(2,1)S(1)} copy(bf16[16,2,4,2560]{0,1,3,2:T(2,128)(2,1)} %bitcast.158) | data formatting | bytes 1310720 | tf_op jit(solution)/shard_map/all_to_all | solution.py:185
  535.8 2.7 fusion.25
  538.5 1.7 fusion.26
  540.2 1.8 fusion.27
  542.0 2.2 add_convert_fusion.6
  544.2 2.8 reshape_reshape.6
  546.9 2.2 add_convert_fusion.5
  549.1 2.8 reshape_reshape.14
  551.9 2.2 add_convert_fusion.4
  554.0 2.8 reshape_reshape.15
  556.8 4.9 fusion.9
  561.8 10.5 %fusion.68 = (f32[2,16,8,32]{3,2,1,0:T(8,128)S(1)}, f32[2,16,8,32,32]{3,4,2,1,0:T(8,128)S(1)}) fusion(f32[2,16,8,32,32]{3,4,2,1,0:T(8,128)S(1)} %fusion.9), kind=kOutput, calls=%fused_computation.142 | output fusion | flops 1048607 | bytes 2129920 | tf_op jit(solution)/shard_map/sub | solution.py:222
  572.3 1.8 convert_bitcast_fusion
  574.2 2.2 copy.143
  576.3 5.8 reshape.328
  582.1 4.2 all-to-all-start.1
  586.3 1.4 copy.145
  587.7 1.9 reshape.330
  589.6 2.6 gather_fusion.1
  592.2 2.7 gather_fusion
  594.9 3.0 copy.127
  597.9 1.6 copy.122
  599.5 1.6 copy.179
  601.8 2.9 fusion.36
  604.6 1.5 convolution_convert_fusion
  606.3 3.5 add_convert_fusion.2
  609.8 1.7 reshape.329
  (132 shorter events, 36.7 us)
Async XLA Ops:
  6.5 204.5 %copy-start = (bf16[320,320]{1,0:T(8,128)(2,1)S(1)}, bf16[320,320]{1,0:T(8,128)(2,1)}, u32[]{:S(2)}) copy-start(bf16[320,320]{1,0:T(8,128)(2,1)} %param.38) | copy-start | bytes 614404
  6.5 21.8 %copy-start.3 = (bf16[16,2,10240]{2,1,0:T(2,128)(2,1)S(1)}, bf16[16,2,10240]{2,1,0:T(2,128)(2,1)}, u32[]{:S(2)}) copy-start(bf16[16,2,10240]{2,1,0:T(2,128)(2,1)} %param.25) | copy-start | bytes 1966084
  30.3 39.9 %copy-start.14 = (f32[320]{0:T(512)S(1)}, f32[320]{0:T(512)}, u32[]{:S(2)}) copy-start(f32[320]{0:T(512)} %param.29) | copy-start | bytes 3844
  30.3 39.9 %copy-start.15 = (f32[320]{0:T(512)S(1)}, f32[320]{0:T(512)}, u32[]{:S(2)}) copy-start(f32[320]{0:T(512)} %param.28) | copy-start | bytes 3844
  70.1 4.9 copy-start.13
  72.2 4.8 collective-permute-start
  73.5 3.6 collective-permute-start.1
  89.1 33.3 %copy-start.23 = (f32[320]{0:T(512)S(1)}, f32[320]{0:T(512)}, u32[]{:S(2)}) copy-start(f32[320]{0:T(512)} %param.33) | copy-start | bytes 3844
  89.1 33.3 %copy-start.24 = (f32[320]{0:T(512)S(1)}, f32[320]{0:T(512)}, u32[]{:S(2)}) copy-start(f32[320]{0:T(512)} %param.32) | copy-start | bytes 3844
  124.4 6.1 copy-start.12
  125.4 13.5 %collective-permute-start.2 = (bf16[16,1,32,320]{3,2,1,0:T(8,128)(2,1)}, bf16[16,1,32,320]{3,2,1,0:T(8,128)(2,1)S(1)}, u32[]{:S(2)}, u32[]{:S(2)}) collective-permute-start(bf16[16,1,32,320]{3,2,1,0:T(8,128)(2,1)} %get-tuple-element.89), channel_id=1, source_target_pairs={{0,1},{1,2},{2,3},{3,4},{4,5},{5,6},{6,7},{8,9},{9,10},{10,11},{11... | collective-permute-start | bytes 983048 | tf_op jit(solution)/shard_map/ppermute | solution.py:27
  126.7 12.2 %collective-permute-start.3 = (bf16[16,1,32,320]{3,2,1,0:T(8,128)(2,1)}, bf16[16,1,32,320]{3,2,1,0:T(8,128)(2,1)}, u32[]{:S(2)}, u32[]{:S(2)}) collective-permute-start(bf16[16,1,32,320]{3,2,1,0:T(8,128)(2,1)} %get-tuple-element.90), channel_id=1, source_target_pairs={{1,0},{2,1},{3,2},{4,3},{5,4},{6,5},{7,6},{9,8},{10,9},{11,10},{12... | collective-permute-start | bytes 983048 | tf_op jit(solution)/shard_map/ppermute | solution.py:28
  206.8 4.3 copy-start.16
  206.8 4.3 copy-start.17
  206.8 4.2 copy-start.18
  211.1 4.0 copy-start.19
  211.1 4.0 copy-start.20
  213.9 1.1 copy-start.2
  233.0 11.9 %copy-start.6 = (bf16[1,4,64,320]{3,2,1,0:T(8,128)(2,1)S(1)}, bf16[1,4,64,320]{3,2,1,0:T(8,128)(2,1)}, u32[]{:S(2)}) copy-start(bf16[1,4,64,320]{3,2,1,0:T(8,128)(2,1)} %param.45) | copy-start | bytes 491524
  233.0 11.9 %copy-start.7 = (bf16[2,4,320,64]{3,2,1,0:T(8,128)(2,1)S(1)}, bf16[2,4,320,64]{3,2,1,0:T(8,128)(2,1)}, u32[]{:S(2)}) copy-start(bf16[2,4,320,64]{3,2,1,0:T(8,128)(2,1)} %custom-call.4) | copy-start | bytes 983044
  233.0 11.9 %copy-start.25 = (s32[2]{0:T(128)S(1)}, s32[2]{0:T(128)}, u32[]{:S(2)}) copy-start(s32[2]{0:T(128)} %param.26) | copy-start | bytes 28
  233.0 11.9 %copy-start.26 = (s32[2]{0:T(128)S(1)}, s32[2]{0:T(128)}, u32[]{:S(2)}) copy-start(s32[2]{0:T(128)} %param.27) | copy-start | bytes 28
  240.5 275.9 %all-to-all-start = ((bf16[4,2,40960]{2,1,0:T(2,128)(2,1)}), bf16[4,2,40960]{2,1,0:T(2,128)(2,1)}, u32[]{:S(2)}, u32[]{:S(2)}) async-start(bf16[4,2,40960]{2,1,0:T(2,128)(2,1)} %reshape.361), calls=%async_computation | async-start | bytes 1310720 | tf_op jit(solution)/shard_map/all_to_all | solution.py:185
  244.9 133.0 %all-reduce.10.cloned.1.call-start = ((), (), s32[]{:S(2)}) async-start(), calls=%async_computation.2 | async-start | bytes 1048576 | tf_op jit(solution)/shard_map/while/body/eval_jaxpr/psum | solution.py:35
  380.0 133.3 %all-reduce.10.cloned.1.call-start = ((), (), s32[]{:S(2)}) async-start(), calls=%async_computation.2 | async-start | bytes 1048576 | tf_op jit(solution)/shard_map/while/body/eval_jaxpr/psum | solution.py:35
  515.3 7.0 %copy-start.8 = (bf16[2,4,320,64]{3,2,1,0:T(8,128)(2,1)}, bf16[2,4,320,64]{3,2,1,0:T(8,128)(2,1)S(1)}, u32[]{:S(2)}) copy-start(bf16[2,4,320,64]{3,2,1,0:T(8,128)(2,1)S(1)} %get-tuple-element.43) | copy-start | bytes 983044
  535.8 2.7 copy-start.10
  561.8 10.5 %copy-start.9 = (bf16[2,32,16,8,40]{4,3,2,1,0:T(8,128)(2,1)S(1)}, bf16[2,32,16,8,40]{4,3,2,1,0:T(8,128)(2,1)}, u32[]{:S(2)}) copy-start(bf16[2,32,16,8,40]{4,3,2,1,0:T(8,128)(2,1)} %reshape_reshape.6) | copy-start | bytes 1966084
  576.3 11.3 %copy-start.4 = (bf16[16,2,10240]{2,1,0:T(2,128)(2,1)S(1)}, bf16[16,2,10240]{2,1,0:T(2,128)(2,1)}, u32[]{:S(2)}) copy-start(bf16[16,2,10240]{2,1,0:T(2,128)(2,1)} %param.25) | copy-start | bytes 1966084
  582.1 17.4 %all-to-all-start.1 = ((bf16[64,2,2560]{2,1,0:T(2,128)(2,1)}), bf16[64,2,2560]{2,1,0:T(2,128)(2,1)}, u32[]{:S(2)}, u32[]{:S(2)}) async-start(bf16[64,2,2560]{2,1,0:T(2,128)(2,1)} %reshape.328), calls=%async_computation.1 | async-start | bytes 1310720 | tf_op jit(solution)/shard_map/all_to_all | solution.py:230
  601.7 4.5 copy-start.5
  601.8 4.5 copy-start.11
  601.8 4.5 copy-start.21
  601.8 4.4 copy-start.22
  606.2 5.2 copy-start.1
Sparse Core Ops, SparseCore 0:
  251.0 126.8 all-reduce.9
  386.1 127.1 all-reduce.9
where the time goes:
time: 626 us; the launch traced here: 619 us
  waiting for transfers between devices  258 us (41%)
  local copies, waits for them, and re-layouts  149 us (24%)
  blocking collectives  88.1 us (14%)
  other arithmetic  57.5 us (9%)
  matrix products  35.6 us (6%)
  starting transfers between devices  14.5 us (2%)
  between operations  14.5 us (2%)
    psum x2, waiting for transfers between devices, spread(): return lax.psum(block, axis)  258 us
    psum x3, blocking collectives, group_stats(): total_one, total_two = lax.psum((leading_entry, second), 'rows')  88.1 us
    convert_element_type x5, local copies, waits for them, and re-layouts, per_device(): xfloat = xin.astype(jnp.float32)  30.4 us
    reduce_sum x3, other arithmetic, group_stats(): leading_entry = jnp.sum(parts, axis=(1, 3))  23.8 us
    unnamed x57, local copies, waits for them, and re-layouts  15.6 us
    reshape x3, local copies, waits for them, and re-layouts, conv_valid(): return total.reshape(frames, extent - 2, W, FEATURE_WIDTH)  15.1 us
    all_to_all x2, local copies, waits for them, and re-layouts, per_device(): lax.all_to_all(normal_in.reshape(frames, strip, W * FEATURE_WIDTH), 'tm',...  12.7 us
  transfers between devices with their start and end apart: 8, of which 3 were waited for; matrix products, arithmetic and copies ran while one was open for 6% of the time, Pallas kernels for 0%

commit v1 on v0

v1 whole, which is shorter than its diff:
```python
import functools
import math

import jax
import jax.numpy as jnp
import numpy as np
from jax import lax
from jax.experimental import pallas as pl
from jax.experimental.pallas import tpu as pltpu
from jax.sharding import PartitionSpec as P

C = 320
GROUPS = 32
GS = 10
HEADS = 8
RANK = 64
W = 32
CLIP_LEN = 32
HD = 40
EPS = 1e-05
F = 16
PIECE = 16
PANEL_ROWS = 8 * RANK
CHUNK = 16
SUB = 8
MESH = pl.DeviceIdType.MESH
F32 = jnp.float32
BF16 = jnp.bfloat16
EXACT = lax.Precision.HIGHEST


def positions():
    index = np.arange(C)
    freq = np.exp(-(index // 2 * 2) * (math.log(10000.0) / C))
    angle = np.arange(CLIP_LEN)[:, None] * freq[None, :]
    return np.where(index[None, :] % 2 == 0, np.sin(angle), np.cos(angle)).astype(np.float32)


def dot(a, b, dims=((1,), (0,)), precision=None):
    return lax.dot_general(a, b, (dims, ((), ())), preferred_element_type=F32, precision=precision)


def silu(v):
    return 0.5 * v * (1.0 + jnp.tanh(0.5 * v))


def kernel(
    nt, nr, strip, clips,
    choice, degrees,
    xt, vec, pe, k1, k2, wi, wa, wo, panel,
    out,
    xs, xh, hs, hh, act, res, proj, nown, npart, ssrc, sland, land1, src2, land2, weff, ot, att,
    hx_s, hx_r, hh_s, hh_r, st_s, st_r, l1_s, l1_r, l2_s, l2_r, n_s, n_r,
):
    n = nt * nr
    pieces = PANEL_ROWS // PIECE
    holders = min(pieces, n)
    my_t = lax.axis_index("tm")
    my_r = lax.axis_index("rows")
    me = my_t * nr + my_r
    side = lax.rem(my_t, 2)
    partner = my_t + 1 - 2 * side
    my_clip = my_t // 2
    count = float(strip * nr * W * GS)
    has_up = my_r > 0
    has_down = my_r < nr - 1

    barrier = pltpu.get_barrier_semaphore()

    def greet(off, carry):
        dst = lax.rem(me + off, n)
        pl.semaphore_signal(barrier, inc=1, device_id=(dst // nr, lax.rem(dst, nr)), device_id_type=MESH)
        return carry

    lax.fori_loop(1, n, greet, 0)

    row = lambda i: vec[i : i + 1, :]
    gc = lax.broadcasted_iota(jnp.int32, (C, 128), 0)
    gg = lax.broadcasted_iota(jnp.int32, (C, 128), 1) * GS
    to_first = ((gc >= gg) & (gc < gg + GS)).astype(F32)
    gg2 = gg - GROUPS * GS
    to_second = ((gc >= gg2) & (gc < gg2 + GS)).astype(F32)

    def unpack(p, carry):
        total, square = carry
        for r in range(strip):
            two = xt[r, :, pl.ds(pl.multiple_of(p * 2 * C, 128), 2 * C)]
            for i in range(2):
                one = two[:, i * C : (i + 1) * C]
                xs[r, 2 * p + i] = one
                wide = one.astype(F32)
                total = total + wide
                square = square + wide * wide
        return total, square

    zero = jnp.zeros((F, C), F32)

    def stat_copy(i, off):
        dst = lax.rem(my_r + off, nr)
        return pltpu.make_async_remote_copy(
            src_ref=ssrc.at[i], dst_ref=sland.at[i, my_r],
            send_sem=st_s.at[i, off], recv_sem=st_r.at[i, my_r],
            device_id=(my_t, dst), device_id_type=MESH)

    def stat_wait(i, off):
        src = lax.rem(my_r + off, nr)
        return pltpu.make_async_remote_copy(
            src_ref=ssrc.at[i], dst_ref=sland.at[i, src],
            send_sem=st_s.at[i, off], recv_sem=st_r.at[i, src],
            device_id=(my_t, src), device_id_type=MESH)

    def put_stats(i, total, square):
        mine = dot(total, to_first, precision=EXACT) + dot(square, to_second, precision=EXACT)
        ssrc[i] = mine
        sland[i, my_r] = mine

    def send_stats(i):
        def step(off, carry):
            stat_copy(i, off).start()
            return carry
        lax.fori_loop(1, nr, step, 0)

    def get_stats(i, gain, shift):
        def step(off, carry):
            stat_wait(i, off).wait_recv()
            return carry
        lax.fori_loop(1, nr, step, 0)
        total = sland[i, 0]
        for s in range(1, nr):
            total = total + sland[i, s]
        total = total * (1.0 / count)
        mean = dot(total, to_first, ((1,), (1,)), EXACT)
        var = dot(total, to_second, ((1,), (1,)), EXACT) - mean * mean
        scale = lax.rsqrt(var + EPS) * gain
        return scale, shift - mean * scale

    def halo(src, dst, send, recv, up):
        if up:
            return pltpu.make_async_remote_copy(
                src_ref=src.at[0], dst_ref=dst.at[1], send_sem=send.at[0], recv_sem=recv.at[1],
                device_id=(my_t, my_r - 1), device_id_type=MESH)
        return pltpu.make_async_remote_copy(
            src_ref=src.at[strip - 1], dst_ref=dst.at[0], send_sem=send.at[1], recv_sem=recv.at[0],
            device_id=(my_t, my_r + 1), device_id_type=MESH)

    def halo_got(src, dst, send, recv, up):
        slot = 0 if up else 1
        return pltpu.make_async_remote_copy(
            src_ref=src.at[0], dst_ref=dst.at[slot], send_sem=send.at[slot], recv_sem=recv.at[slot],
            device_id=(my_t, my_r - 1 if up else my_r + 1), device_id_type=MESH)

    def send_halo(src, dst, send, recv):
        @pl.when(has_up)
        def _():
            halo(src, dst, send, recv, True).start()

        @pl.when(has_down)
        def _():
            halo(src, dst, send, recv, False).start()

    def halo_sent(src, dst, send, recv):
        @pl.when(has_up)
        def _():
            halo(src, dst, send, recv, True).wait_send()

        @pl.when(has_down)
        def _():
            halo(src, dst, send, recv, False).wait_send()

    def activate(src, edges, send, recv, scale, shift):
        def one(value):
            return silu(value.astype(F32) * scale + shift).astype(BF16)

        def body(w, carry):
            for r in range(strip):
                act[r + 1, w + 1] = one(src[r, w])
            return carry

        lax.fori_loop(0, W, body, 0, unroll=4)
        for up in (True, False):
            there = has_up if up else has_down
            slot, line = (0, 0) if up else (1, strip + 1)

            @pl.when(there)
            def _():
                halo_got(src, edges, send, recv, up).wait_recv()

                def edge(w, carry):
                    act[line, w + 1] = one(edges[slot, w])
                    return carry

                lax.fori_loop(0, W, edge, 0, unroll=4)

            @pl.when(jnp.logical_not(there))
            def _():
                act[line, 1 : W + 1] = jnp.zeros((W, F, C), BF16)

    def conv(r, weight):
        total = None
        for dy in range(3):
            for dx in range(3):
                window = act[r + dy, dx : dx + W].reshape(W * F, C)
                term = dot(window, weight[3 * dy + dx])
                total = term if total is None else total + term
        return total

    total, square = lax.fori_loop(0, W // 2, unpack, (zero, zero))
    put_stats(0, total, square)
    for r in range(strip + 2):
        act[r, 0] = jnp.zeros((F, C), BF16)
        act[r, W + 1] = jnp.zeros((F, C), BF16)
    pl.semaphore_wait(barrier, n - 1)
    send_stats(0)
    send_halo(xs, xh, hx_s, hx_r)

    def piece_copy(p):
        return pltpu.make_async_remote_copy(
            src_ref=panel.at[pl.ds(pl.multiple_of(p * PIECE, PIECE), PIECE)], dst_ref=land1.at[me],
            send_sem=l1_s.at[p], recv_sem=l1_r.at[me],
            device_id=(p // nr, lax.rem(p, nr)), device_id_type=MESH)

    def piece_start(off, carry):
        p = lax.rem(me + off, n)

        @pl.when(p < holders)
        def _():
            piece_copy(p).start()
        return carry

    lax.fori_loop(1, n, piece_start, 0)

    @pl.when(me < holders)
    def _():
        land1[me] = panel[pl.ds(pl.multiple_of(me * PIECE, PIECE), PIECE)]

    scale, shift = get_stats(0, row(0), row(1))
    activate(xs, xh, hx_s, hx_r, scale, shift)

    def conv_one(r, carry):
        total, square = carry
        value = (conv(r, k1) + row(2)).astype(BF16)
        hs[r] = value.reshape(W, F, C)
        wide = value.astype(F32).reshape(W, F, C)
        return total + jnp.sum(wide, axis=0), square + jnp.sum(wide * wide, axis=0)

    total, square = lax.fori_loop(0, strip, conv_one, (zero, zero))
    send_halo(hs, hh, hh_s, hh_r)
    put_stats(1, total, square)
    send_stats(1)

    def share_copy(dst):
        return pltpu.make_async_remote_copy(
            src_ref=src2.at[(dst // nr) // 2], dst_ref=land2.at[me],
            send_sem=l2_s.at[dst], recv_sem=l2_r.at[me],
            device_id=(dst // nr, lax.rem(dst, nr)), device_id_type=MESH)

    @pl.when(me < holders)
    def _():
        def piece_wait(off, carry):
            s = lax.rem(me + off, n)
            pltpu.make_async_remote_copy(
                src_ref=panel.at[pl.ds(0, PIECE)], dst_ref=land1.at[s],
                send_sem=l1_s.at[0], recv_sem=l1_r.at[s],
                device_id=(s // nr, lax.rem(s, nr)), device_id_type=MESH).wait_recv()
            return carry

        lax.fori_loop(1, n, piece_wait, 0)
        for k in range(clips):
            src2[k] = land1[choice[k]]
        land2[me] = src2[my_clip]

        def share(off, carry):
            share_copy(lax.rem(me + off, n)).start()
            return carry

        lax.fori_loop(1, n, share, 0)

    scale, shift = get_stats(1, row(3), row(4))
    activate(hs, hh, hh_s, hh_r, scale, shift)

    def conv_two(r, carry):
        total, square = carry
        value = conv(r, k2) + xs[r].reshape(W * F, C).astype(F32) + row(5)
        value = value.astype(BF16)
        res[r] = value.reshape(W, F, C)
        wide = value.astype(F32).reshape(W, F, C)
        return total + jnp.sum(wide, axis=0), square + jnp.sum(wide * wide, axis=0)

    total, square = lax.fori_loop(0, strip, conv_two, (zero, zero))
    put_stats(2, total, square)
    send_stats(2)

    def share_wait(off, carry):
        s = lax.rem(me + off, n)

        @pl.when(s < holders)
        def _():
            pltpu.make_async_remote_copy(
                src_ref=src2.at[0], dst_ref=land2.at[s],
                send_sem=l2_s.at[0], recv_sem=l2_r.at[s],
                device_id=(s // nr, lax.rem(s, nr)), device_id_type=MESH).wait_recv()
        return carry

    lax.fori_loop(1, n, share_wait, 0)
    degree = degrees[my_clip]
    kept = lax.broadcasted_iota(jnp.int32, (RANK, C), 0) < degree
    per = RANK // PIECE
    for j in range(4):
        down = land2[j * per : (j + 1) * per].reshape(RANK, C)
        down = jnp.where(kept, down.astype(F32), 0.0).astype(BF16)
        up = land2[(4 + j) * per : (5 + j) * per].reshape(RANK, C)
        pair = (up, down) if j == 2 else (down, up)
        weff[j] = (wa[j].astype(F32) + dot(pair[0], pair[1], ((0,), (0,)))).astype(BF16)

    scale, shift = get_stats(2, row(6), row(7))
    stamp = pe[pl.ds(pl.multiple_of(side * F, F), F)] + row(10)
    chunks = strip * W // CHUNK
    per_row = W // CHUNK

    def chunk_copy(c):
        return pltpu.make_async_remote_copy(
            src_ref=nown.at[c], dst_ref=npart.at[c], send_sem=n_s.at[c], recv_sem=n_r.at[c],
            device_id=(partner, my_r), device_id_type=MESH)

    def project(c, carry):
        r, w0 = c // per_row, lax.rem(c, per_row) * CHUNK
        u = (res[r, pl.ds(w0, CHUNK)].astype(F32) * scale + shift).astype(BF16)
        p = (dot(u.reshape(CHUNK * F, C), wi[...]) + row(8)).astype(BF16)
        proj[c] = p
        p = p.astype(F32)
        centre = p - jnp.sum(p, axis=-1, keepdims=True) * (1.0 / C)
        var = jnp.sum(centre * centre, axis=-1, keepdims=True) * (1.0 / C)
        layer = centre * lax.rsqrt(var + EPS) * row(9)
        layer = layer.reshape(CHUNK, F, C) + stamp
        nown[c] = layer.astype(BF16).reshape(CHUNK * F, C)
        chunk_copy(c).start()
        return carry

    lax.fori_loop(0, chunks, project, 0)

    rows = SUB * F
    key_pixel = lax.rem(lax.broadcasted_iota(jnp.int32, (2 * rows, rows), 0), rows) // F
    query_pixel = lax.broadcasted_iota(jnp.int32, (2 * rows, rows), 1) // F
    same = key_pixel == query_pixel
    lane = lax.broadcasted_iota(jnp.int32, (1, C), 1)
    root = 1.0 / math.sqrt(HD)

    def attend(c, carry):
        r, w0 = c // per_row, lax.rem(c, per_row) * CHUNK
        chunk_copy(c).wait_recv()
        for s in range(CHUNK // SUB):
            mine = nown[c, s * rows : (s + 1) * rows]
            theirs = npart[c, s * rows : (s + 1) * rows]
            both = jnp.concatenate([mine, theirs], axis=0)
            query = dot(mine, weff[0]).astype(BF16)
            keys = dot(both, weff[1]).astype(BF16)
            vals = dot(weff[2], both, ((1,), (1,))).astype(BF16).astype(F32)
            for h in range(HEADS):
                head = ((lane >= h * HD) & (lane < (h + 1) * HD)).astype(BF16)
                scores = dot(keys * head, query, ((1,), (1,)))
                scores = jnp.where(same, scores * root, -1e30)
                top = jnp.max(scores, axis=0, keepdims=True)
                power = jnp.exp(scores - top)
                total = jnp.sum(power, axis=0, keepdims=True)
                weights = (power * (1.0 / total)).astype(BF16)
                ot[h * HD : (h + 1) * HD, s * rows : (s + 1) * rows] = dot(
                    vals[h * HD : (h + 1) * HD].astype(BF16), weights)
        y = dot(ot[...].astype(BF16), weff[3], ((0,), (0,)))
        y = (y + proj[c].astype(F32) + row(11)).astype(BF16)
        final = dot(y, wo[...]) + res[r, pl.ds(w0, CHUNK)].reshape(CHUNK * F, C).astype(F32) + row(12)
        final = final.astype(BF16).reshape(CHUNK, F, C)
        for p in range(CHUNK // 2):
            two = jnp.concatenate([final[2 * p], final[2 * p + 1]], axis=-1)
            out[r, :, pl.ds(pl.multiple_of((w0 + 2 * p) * C, 128), 2 * C)] = two
        return carry

    lax.fori_loop(0, chunks, attend, 0)

    def sent(c, carry):
        chunk_copy(c).wait_send()
        return carry

    lax.fori_loop(0, chunks, sent, 0)
    for i in range(3):
        def step(off, carry):
            stat_copy(i, off).wait_send()
            return carry
        lax.fori_loop(1, nr, step, 0)
    halo_sent(xs, xh, hx_s, hx_r)
    halo_sent(hs, hh, hh_s, hh_r)

    def piece_sent(off, carry):
        p = lax.rem(me + off, n)

        @pl.when(p < holders)
        def _():
            piece_copy(p).wait_send()
        return carry

    lax.fori_loop(1, n, piece_sent, 0)

    @pl.when(me < holders)
    def _():
        def share_sent(off, carry):
            share_copy(lax.rem(me + off, n)).wait_send()
            return carry

        lax.fori_loop(1, n, share_sent, 0)


def per_device(
    latents, choice, degrees,
    gain1, shift1, k1, bias1, gain2, shift2, k2, bias2, gain3, shift3,
    wi, bi, ln_gain, ln_shift, wa, ab, lower, raise_, wo, ob,
):
    nt, nr = lax.axis_size("tm"), lax.axis_size("rows")
    n = nt * nr
    strip = latents.shape[1]
    clips = choice.shape[0]
    xt = jnp.transpose(latents, (1, 0, 2))
    vec = jnp.stack([gain1, shift1, bias1, gain2, shift2, bias2, gain3, shift3, bi, ln_gain, ln_shift, ab, ob])
    panel = jnp.concatenate(
        [jnp.transpose(lower[0], (0, 2, 1)).reshape(-1, C), raise_[0].reshape(-1, C)], axis=0)
    wa = jnp.stack([wa[0], wa[1], wa[2].T, wa[3]])
    vmem = pl.BlockSpec(memory_space=pltpu.VMEM)
    smem = pl.BlockSpec(memory_space=pltpu.SMEM)
    chunks = strip * W // CHUNK
    holders = min(PANEL_ROWS // PIECE, n)
    dma = pltpu.SemaphoreType.DMA
    out = pl.pallas_call(
        functools.partial(kernel, nt, nr, strip, clips),
        out_shape=jax.ShapeDtypeStruct(xt.shape, BF16),
        in_specs=[smem, smem] + [vmem] * 9,
        out_specs=vmem,
        scratch_shapes=[
            pltpu.VMEM((strip, W, F, C), BF16),
            pltpu.VMEM((2, W, F, C), BF16),
            pltpu.VMEM((strip, W, F, C), BF16),
            pltpu.VMEM((2, W, F, C), BF16),
            pltpu.VMEM((strip + 2, W + 2, F, C), BF16),
            pltpu.VMEM((strip, W, F, C), BF16),
            pltpu.VMEM((chunks, CHUNK * F, C), BF16),
            pltpu.VMEM((chunks, CHUNK * F, C), BF16),
            pltpu.VMEM((chunks, CHUNK * F, C), BF16),
            pltpu.VMEM((3, F, 128), F32),
            pltpu.VMEM((3, nr, F, 128), F32),
            pltpu.VMEM((n, PIECE, C), BF16),
            pltpu.VMEM((clips, PIECE, C), BF16),
            pltpu.VMEM((holders, PIECE, C), BF16),
            pltpu.VMEM((4, C, C), BF16),
            pltpu.VMEM((C, CHUNK * F), F32),
            pltpu.VMEM((8, 128), F32),
            dma((2,)), dma((2,)), dma((2,)), dma((2,)),
            dma((3, nr)), dma((3, nr)),
            dma((holders,)), dma((n,)), dma((n,)), dma((holders,)),
            dma((chunks,)), dma((chunks,)),
        ],
        compiler_params=pltpu.CompilerParams(
            collective_id=0, has_side_effects=True, vmem_limit_bytes=48 * 1024 * 1024),
        cost_estimate=pl.CostEstimate(flops=6 * 10**9, bytes_accessed=8 * 10**6, transcendentals=3 * 10**6),
    )(choice, degrees, xt, vec, jnp.asarray(positions()), k1.reshape(9, C, C), k2.reshape(9, C, C), wi, wa, wo, panel)
    return jnp.transpose(out, (1, 0, 2))


def solution(mesh):
    everywhere = P()
    in_specs = (
        (P("tm", "rows", None),) + (everywhere,) * 18
        + (P(("tm", "rows"), None, None, None),) * 2 + (everywhere,) * 2
    )
    return jax.shard_map(
        per_device, mesh=mesh, in_specs=in_specs, out_specs=P("tm", "rows", None), check_vma=False
    )
```

time: 626 us -> 101 us (0.16); the launches traced: 619 us -> 101 us
  waiting for transfers between devices: 258 us -> 0 us
  local copies, waits for them, and re-layouts: 149 us -> 15.7 us
  blocking collectives: 88.1 us -> 0 us
  Pallas kernels: 0 us -> 82.2 us
  other arithmetic: 57.5 us -> 2.49 us
  matrix products: 35.6 us -> 0 us
  starting transfers between devices: 14.5 us -> 0 us
  between operations: 14.5 us -> 0.12 us
    psum x2 -> x0, waiting for transfers between devices: 258 us -> none  [spread(): return lax.psum(block, axis)]
    psum x3 -> x0, blocking collectives: 88.1 us -> none  [group_stats(): total_one, total_two = lax.psum((leading_entry, second), 'rows')]
    pallas_call x0 -> x1, Pallas kernels: none -> 82.2 us  [per_device(): pl.pallas_call(functools.partial(kernel, nt, nr, strip, clips), out_shape...]
    convert_element_type x8 -> x0, local copies, waits for them, and re-layouts: 43.6 us -> none  [the longest x5 30.4 us: per_device(): xfloat = xin.astype(jnp.float32)]
    dot_general x18 -> x0, matrix products: 35.6 us -> none  [the longest x3 6.51 us: remote_project(): jnp.dot(rank_limited.reshape(-1, FEATURE_WIDTH), attention_weight[project...]
    reshape x6 -> x0, local copies, waits for them, and re-layouts: 25.8 us -> none  [the longest x3 15.1 us: conv_valid(): return total.reshape(frames, extent - 2, W, FEATURE_WIDTH)]
    reduce_sum x4 -> x0, other arithmetic: 23.9 us -> none  [the longest x3 23.8 us: group_stats(): leading_entry = jnp.sum(parts, axis=(1, 3))]
    all_to_all x3 -> x0, local copies, waits for them, and re-layouts: 14.3 us -> none  [the longest x2 12.7 us: per_device(): lax.all_to_all(normal_in.reshape(frames, strip, W * FEATURE_WIDTH), 'tm',...]
  transfers between devices with their start and end apart: 8 -> 0, of which waited for: 3 -> 0; matrix products, arithmetic and copies ran while one was open for 6% -> 0% of each run, Pallas kernels for 0% -> 0%
where the time goes in v1:
time: 101 us
  Pallas kernels  82.2 us (81%)
  local copies, waits for them, and re-layouts  15.7 us (16%)
  other arithmetic  2.49 us (2%)
    pallas_call x1, Pallas kernels, per_device(): pl.pallas_call(functools.partial(kernel, nt, nr, strip, clips), out_shape...  82.2 us
    another operation x14, local copies, waits for them, and re-layouts, per_device(): jnp.stack([gain1, shift1, bias1, gain2, shift2, bias2, gain3, shift3, bi,...  8.93 us
    slice x2, local copies, waits for them, and re-layouts, per_device(): wa = jnp.stack([wa[0], wa[1], wa[2].T, wa[3]])  3.9 us

profile of v1, /device:TPU:0, one launch (start us, length us, event | category | flops | bytes accessed | tf_op | source)
XLA Modules:
  0.0 100.5 jit_solution(3756789896649819648)
XLA Ops:
  0.0 0.7 stack.48
  0.7 0.7 stack.49
  1.4 0.7 stack.50
  2.0 0.7 stack.51
  2.7 0.7 stack.52
  3.4 0.7 stack.53
  4.1 0.7 stack.54
  4.8 0.7 stack.55
  5.5 0.7 stack.56
  6.1 0.7 stack.57
  6.8 0.7 stack.58
  7.5 0.7 stack.59
  8.2 0.7 stack.60
  8.9 0.1 stack.61.vec
  8.9 1.1 %pad_maximum_fusion.1.panel = bf16[512,320]{1,0:T(8,128)(2,1)S(1)} fusion(bf16[256,320]{1,0:T(8,128)(2,1)} %bitcast.21, bf16[256,320]{1,0:T(8,128)(2,1)} %bitcast.22), kind=kLoop, calls=%fused_computation.2 | loop fusion | flops 655360 | bytes 655360 | tf_op jit(solution)/shard_map/concatenate | solution.py:422
  10.0 1.9 %slice.11 = bf16[2,320,320]{2,1,0:T(8,128)(2,1)} slice(bf16[4,320,320]{2,1,0:T(8,128)(2,1)} %param.41), slice={[0:2], [0:320], [0:320]} | slice | bytes 819200 | tf_op jit(solution)/shard_map/slice | solution.py:424
  11.9 0.0 copy-start
  11.9 0.0 copy-start.1
  11.9 0.0 copy-start.2
  11.9 0.0 copy-start.3
  11.9 0.0 copy-start.4
  11.9 0.0 copy-start.5
  11.9 2.0 %fusion = (bf16[1,320,320]{2,1,0:T(8,128)(2,1)}, bf16[1,320,320]{2,1,0:T(8,128)(2,1)}) fusion(bf16[4,320,320]{2,1,0:T(8,128)(2,1)} %param.41), kind=kLoop, calls=%fused_computation.3 | loop fusion | bytes 819200 | tf_op jit(solution)/shard_map/slice | solution.py:424
  13.9 1.1 %copy.28 = bf16[1,320,320]{1,2,0:T(8,128)(2,1)S(1)} copy(bf16[1,320,320]{2,1,0:T(8,128)(2,1)} %get-tuple-element.5) | data formatting | bytes 409600
  15.1 0.0 copy-start.6
  15.1 1.4 %pad_maximum_fusion.wa = bf16[4,320,320]{2,1,0:T(8,128)(2,1)S(1)} fusion(bf16[1,320,320]{2,1,0:T(8,128)(2,1)} %get-tuple-element.6, bf16[1,320,320]{2,1,0:T(8,128)(2,1)S(1)} %bitcast.20, bf16[2,320,320]{2,1,0:T(8,128)(2,1)} %slice.11), kind=kLoop, calls=%fused_computation | loop fusion | flops 819200 | bytes 1638400 | tf_op jit(solution)/shard_map/stack | solution.py:424
  16.5 0.0 copy-done.6
  16.5 0.2 copy.30
  16.7 0.0 copy-done
  16.7 0.0 copy-done.1
  16.7 0.0 copy-done.2
  16.8 0.0 copy-done.3
  16.8 0.0 copy-done.4
  16.8 0.0 copy-done.5
  16.8 82.2 %shard_map.226 = bf16[2,16,10240]{2,1,0:T(8,128)(2,1)S(1)} custom-call(s32[2]{0:T(128)S(1)} %copy-done.3, s32[2]{0:T(128)S(1)} %copy-done.4, bf16[2,16,10240]{2,1,0:T(8,128)(2,1)S(1)} %bitcast.18, f32[13,320]{1,0:T(8,128)S(1)} %stack.61.vec, f32[32,320]{1,0:T(8,128)S(1)} %copy-done.5, bf16[9,320,320]{2,1,0:T(8,128)(2,1)S(1)} %bitcast.19, ...), custom_call_target="tpu_custom_call" | custom-call | flops 6000000000 | bytes 8000000 | tf_op jit(solution)/shard_map/pallas_call | solution.py:430
  99.0 1.5 %copy.27 = bf16[16,2,10240]{2,1,0:T(2,128)(2,1)} copy(bf16[16,2,10240]{2,0,1:T(8,128)(2,1)S(1)} %bitcast.17) | data formatting | bytes 1310720 | tf_op jit(solution)/shard_map/transpose | solution.py:462
Async XLA Ops:
  11.9 4.9 %copy-start = (bf16[3,3,320,320]{3,2,1,0:T(8,128)(2,1)S(1)}, bf16[3,3,320,320]{3,2,1,0:T(8,128)(2,1)}, u32[]{:S(2)}) copy-start(bf16[3,3,320,320]{3,2,1,0:T(8,128)(2,1)} %param.29) | copy-start | bytes 5529604
  11.9 4.9 %copy-start.1 = (bf16[320,320]{1,0:T(8,128)(2,1)S(1)}, bf16[320,320]{1,0:T(8,128)(2,1)}, u32[]{:S(2)}) copy-start(bf16[320,320]{1,0:T(8,128)(2,1)} %wi.1) | copy-start | bytes 614404
  11.9 4.9 %copy-start.2 = (bf16[320,320]{1,0:T(8,128)(2,1)S(1)}, bf16[320,320]{1,0:T(8,128)(2,1)}, u32[]{:S(2)}) copy-start(bf16[320,320]{1,0:T(8,128)(2,1)} %wo.1) | copy-start | bytes 614404
  11.9 4.9 %copy-start.3 = (s32[2]{0:T(128)S(1)}, s32[2]{0:T(128)}, u32[]{:S(2)}) copy-start(s32[2]{0:T(128)} %choice.1) | copy-start | bytes 28
  11.9 4.9 %copy-start.4 = (s32[2]{0:T(128)S(1)}, s32[2]{0:T(128)}, u32[]{:S(2)}) copy-start(s32[2]{0:T(128)} %degrees.1) | copy-start | bytes 28
  11.9 4.9 %copy-start.5 = (f32[32,320]{1,0:T(8,128)S(1)}, f32[32,320]{1,0:T(8,128)}, u32[]{:S(2)}) copy-start(f32[32,320]{1,0:T(8,128)} %constant.2.clone.pe) | copy-start | bytes 122884
  15.1 1.4 %copy-start.6 = (bf16[16,2,10240]{2,1,0:T(2,128)(2,1)S(1)}, bf16[16,2,10240]{2,1,0:T(2,128)(2,1)}, u32[]{:S(2)}) copy-start(bf16[16,2,10240]{2,1,0:T(2,128)(2,1)} %param.24) | copy-start | bytes 1966084

commit v2 on v1

--- a/solution.py
+++ b/solution.py
@@ -47,11 +47,12 @@
 def kernel(
     nt, nr, strip, clips,
     choice, degrees,
-    xt, vec, pe, k1, k2, wi, wa, wo, panel,
-    out,
-    xs, xh, hs, hh, act, res, proj, nown, npart, ssrc, sland, land1, src2, land2, weff, ot, att,
-    hx_s, hx_r, hh_s, hh_r, st_s, st_r, l1_s, l1_r, l2_s, l2_r, n_s, n_r,
+    xt, *refs,
 ):
+    vec, refs = refs[:13], refs[13:]
+    pe, k1, k2, wi, wa, wo, lower, upper, out, *refs = refs
+    xs, xh, hs, hh, act, res, proj, nown, npart, ssrc, sland, land1, src2, land2, weff, ot, *refs = refs
+    hx_s, hx_r, hh_s, hh_r, st_s, st_r, l1_s, l1_r, l2_s, l2_r, n_s, n_r = refs
     n = nt * nr
     pieces = PANEL_ROWS // PIECE
     holders = min(pieces, n)
@@ -74,7 +75,7 @@
 
     lax.fori_loop(1, n, greet, 0)
 
-    row = lambda i: vec[i : i + 1, :]
+    row = lambda i: vec[i][...].reshape(1, C)
     gc = lax.broadcasted_iota(jnp.int32, (C, 128), 0)
     gg = lax.broadcasted_iota(jnp.int32, (C, 128), 1) * GS
     to_first = ((gc >= gg) & (gc < gg + GS)).astype(F32)
@@ -213,25 +214,38 @@
     send_stats(0)
     send_halo(xs, xh, hx_s, hx_r)
 
-    def piece_copy(p):
-        return pltpu.make_async_remote_copy(
-            src_ref=panel.at[pl.ds(pl.multiple_of(p * PIECE, PIECE), PIECE)], dst_ref=land1.at[me],
+    half = pieces // 2
+
+    def rows_of(p):
+        return pl.ds(pl.multiple_of(p * PIECE, PIECE), PIECE)
+
+    def piece_copy(p, panel, first):
+        return pltpu.make_async_remote_copy(
+            src_ref=panel.at[rows_of(p - first)], dst_ref=land1.at[me],
             send_sem=l1_s.at[p], recv_sem=l1_r.at[me],
             device_id=(p // nr, lax.rem(p, nr)), device_id_type=MESH)
 
     def piece_start(off, carry):
         p = lax.rem(me + off, n)
 
-        @pl.when(p < holders)
-        def _():
-            piece_copy(p).start()
+        @pl.when(p < half)
+        def _():
+            piece_copy(p, lower, 0).start()
+
+        @pl.when((p >= half) & (p < holders))
+        def _():
+            piece_copy(p, upper, half).start()
         return carry
 
     lax.fori_loop(1, n, piece_start, 0)
 
-    @pl.when(me < holders)
+    @pl.when(me < half)
     def _():
-        land1[me] = panel[pl.ds(pl.multiple_of(me * PIECE, PIECE), PIECE)]
+        land1[me] = lower[rows_of(me)]
+
+    @pl.when((me >= half) & (me < holders))
+    def _():
+        land1[me] = upper[rows_of(me - half)]
 
     scale, shift = get_stats(0, row(0), row(1))
     activate(xs, xh, hx_s, hx_r, scale, shift)
@@ -259,7 +273,7 @@
         def piece_wait(off, carry):
             s = lax.rem(me + off, n)
             pltpu.make_async_remote_copy(
-                src_ref=panel.at[pl.ds(0, PIECE)], dst_ref=land1.at[s],
+                src_ref=lower.at[pl.ds(0, PIECE)], dst_ref=land1.at[s],
                 send_sem=l1_s.at[0], recv_sem=l1_r.at[s],
                 device_id=(s // nr, lax.rem(s, nr)), device_id_type=MESH).wait_recv()
             return carry
@@ -309,8 +323,8 @@
         down = land2[j * per : (j + 1) * per].reshape(RANK, C)
         down = jnp.where(kept, down.astype(F32), 0.0).astype(BF16)
         up = land2[(4 + j) * per : (5 + j) * per].reshape(RANK, C)
-        pair = (up, down) if j == 2 else (down, up)
-        weff[j] = (wa[j].astype(F32) + dot(pair[0], pair[1], ((0,), (0,)))).astype(BF16)
+        value = wa[j].astype(F32) + dot(down, up, ((0,), (0,)))
+        weff[j] = (value.T if j == 2 else value).astype(BF16)
 
     scale, shift = get_stats(2, row(6), row(7))
     stamp = pe[pl.ds(pl.multiple_of(side * F, F), F)] + row(10)
@@ -394,7 +408,7 @@
 
         @pl.when(p < holders)
         def _():
-            piece_copy(p).wait_send()
+            piece_copy(p, lower, p).wait_send()
         return carry
 
     lax.fori_loop(1, n, piece_sent, 0)
@@ -418,10 +432,9 @@
     strip = latents.shape[1]
     clips = choice.shape[0]
     xt = jnp.transpose(latents, (1, 0, 2))
-    vec = jnp.stack([gain1, shift1, bias1, gain2, shift2, bias2, gain3, shift3, bi, ln_gain, ln_shift, ab, ob])
-    panel = jnp.concatenate(
-        [jnp.transpose(lower[0], (0, 2, 1)).reshape(-1, C), raise_[0].reshape(-1, C)], axis=0)
-    wa = jnp.stack([wa[0], wa[1], wa[2].T, wa[3]])
+    vec = [gain1, shift1, bias1, gain2, shift2, bias2, gain3, shift3, bi, ln_gain, ln_shift, ab, ob]
+    lower = jnp.transpose(lower[0], (0, 2, 1)).reshape(-1, C)
+    upper = raise_[0].reshape(-1, C)
     vmem = pl.BlockSpec(memory_space=pltpu.VMEM)
     smem = pl.BlockSpec(memory_space=pltpu.SMEM)
     chunks = strip * W // CHUNK
@@ -430,7 +443,7 @@
     out = pl.pallas_call(
         functools.partial(kernel, nt, nr, strip, clips),
         out_shape=jax.ShapeDtypeStruct(xt.shape, BF16),
-        in_specs=[smem, smem] + [vmem] * 9,
+        in_specs=[smem, smem] + [vmem] * 22,
         out_specs=vmem,
         scratch_shapes=[
             pltpu.VMEM((strip, W, F, C), BF16),
@@ -449,7 +462,6 @@
             pltpu.VMEM((holders, PIECE, C), BF16),
             pltpu.VMEM((4, C, C), BF16),
             pltpu.VMEM((C, CHUNK * F), F32),
-            pltpu.VMEM((8, 128), F32),
             dma((2,)), dma((2,)), dma((2,)), dma((2,)),
             dma((3, nr)), dma((3, nr)),
             dma((holders,)), dma((n,)), dma((n,)), dma((holders,)),
@@ -458,7 +470,9 @@
         compiler_params=pltpu.CompilerParams(
             collective_id=0, has_side_effects=True, vmem_limit_bytes=48 * 1024 * 1024),
         cost_estimate=pl.CostEstimate(flops=6 * 10**9, bytes_accessed=8 * 10**6, transcendentals=3 * 10**6),
-    )(choice, degrees, xt, vec, jnp.asarray(positions()), k1.reshape(9, C, C), k2.reshape(9, C, C), wi, wa, wo, panel)
+    )(
+        choice, degrees, xt, *vec, jnp.asarray(positions()),
+        k1.reshape(9, C, C), k2.reshape(9, C, C), wi, wa, wo, lower, upper)
     return jnp.transpose(out, (1, 0, 2))
 
 

time: 101 us -> 103 us (1.020)
  local copies, waits for them, and re-layouts: 15.7 us -> 20.3 us
  other arithmetic: 2.49 us -> 0 us
    unnamed x16 -> x45, local copies, waits for them, and re-layouts: 1.36 us -> 18.8 us
    another operation x14 -> x0, local copies, waits for them, and re-layouts: 8.93 us -> none  [per_device(): jnp.stack([gain1, shift1, bias1, gain2, shift2, bias2, gain3, shift3, bi,...]
    slice x2 -> x0, local copies, waits for them, and re-layouts: 3.9 us -> none  [per_device(): wa = jnp.stack([wa[0], wa[1], wa[2].T, wa[3]])]
    another operation x1 -> x0, other arithmetic: 1.43 us -> none  [per_device(): wa = jnp.stack([wa[0], wa[1], wa[2].T, wa[3]])]
    concatenate x1 -> x0, other arithmetic: 1.07 us -> none  [per_device(): jnp.concatenate([jnp.transpose(lower[0], (0, 2, 1)).reshape(-1, C), raise...]
where the time goes in v2:
time: 103 us
  Pallas kernels  82.2 us (80%)
  local copies, waits for them, and re-layouts  20.3 us (20%)
    pallas_call x1, Pallas kernels, per_device(): pl.pallas_call(functools.partial(kernel, nt, nr, strip, clips), out_shape...  82.2 us
    unnamed x45, local copies, waits for them, and re-layouts  18.8 us

profile of v2, /device:TPU:0, one launch (start us, length us, event | category | flops | bytes accessed | tf_op | source)
XLA Modules:
  0.0 102.6 jit_solution(13912845024547738689)
XLA Ops:
  0.0 1.3 %copy.28 = bf16[16,2,10240]{2,0,1:T(8,128)(2,1)S(1)} copy(bf16[16,2,10240]{2,1,0:T(2,128)(2,1)} %param.24) | data formatting | bytes 1310720 | tf_op args[0]
  1.3 0.0 copy-start
  1.3 1.6 %copy-done = bf16[3,3,320,320]{3,2,1,0:T(8,128)(2,1)S(1)} copy-done((bf16[3,3,320,320]{3,2,1,0:T(8,128)(2,1)S(1)}, bf16[3,3,320,320]{3,2,1,0:T(8,128)(2,1)}, u32[]{:S(2)}) %copy-start) | copy-done | bytes 1843224
  2.9 0.0 copy-start.1
  2.9 1.2 %copy-done.1 = bf16[4,320,320]{2,1,0:T(8,128)(2,1)S(1)} copy-done((bf16[4,320,320]{2,1,0:T(8,128)(2,1)S(1)}, bf16[4,320,320]{2,1,0:T(8,128)(2,1)}, u32[]{:S(2)}) %copy-start.1) | copy-done | bytes 819224
  4.1 0.0 copy-start.2
  4.1 0.9 copy-done.2
  5.1 0.0 copy-start.3
  5.1 0.9 copy-done.3
  6.0 0.0 copy-start.4
  6.0 0.9 copy-done.4
  6.9 0.0 copy-start.5
  6.9 0.9 copy-done.5
  7.9 0.0 copy-start.6
  7.9 0.7 copy-done.6
  8.5 0.0 copy-start.7
  8.5 0.7 copy-done.7
  9.2 0.0 copy-start.8
  9.2 0.7 copy-done.8
  9.9 0.0 copy-start.9
  9.9 0.7 copy-done.9
  10.6 0.0 copy-start.10
  10.6 0.7 copy-done.10
  11.3 0.0 copy-start.11
  11.3 0.7 copy-done.11
  11.9 0.0 copy-start.12
  12.0 0.7 copy-done.12
  12.6 0.0 copy-start.13
  12.6 0.7 copy-done.13
  13.3 0.0 copy-start.14
  13.3 0.7 copy-done.14
  14.0 0.0 copy-start.15
  14.0 0.7 copy-done.15
  14.7 0.0 copy-start.16
  14.7 0.7 copy-done.16
  15.4 0.0 copy-start.17
  15.4 0.7 copy-done.17
  16.0 0.0 copy-start.18
  16.0 0.7 copy-done.18
  16.7 0.0 copy-start.19
  16.7 0.7 copy-done.19
  17.4 0.0 copy-start.20
  17.4 0.7 copy-done.20
  18.0 0.0 copy-start.21
  18.0 0.8 copy-done.21
  18.8 82.2 %shard_map.226 = bf16[2,16,10240]{2,1,0:T(8,128)(2,1)S(1)} custom-call(s32[2]{0:T(128)S(1)} %copy-done.19, s32[2]{0:T(128)S(1)} %copy-done.20, bf16[2,16,10240]{2,1,0:T(8,128)(2,1)S(1)} %bitcast.13, f32[320]{0:T(512)S(1)} %copy-done.6, f32[320]{0:T(512)S(1)} %copy-done.7, f32[320]{0:T(512)S(1)} %copy-done.8, f32[320]{0:T(512)S(1)} %copy-done.9, ...), custom_call_target="tpu_custom_call" | custom-call | flops 6000000000 | bytes 8000000 | tf_op jit(solution)/shard_map/pallas_call | solution.py:443
  101.1 1.5 %copy.26 = bf16[16,2,10240]{2,1,0:T(2,128)(2,1)} copy(bf16[16,2,10240]{2,0,1:T(8,128)(2,1)S(1)} %bitcast.12) | data formatting | bytes 1310720 | tf_op jit(solution)/shard_map/transpose | solution.py:476
Async XLA Ops:
  1.3 1.6 %copy-start = (bf16[3,3,320,320]{3,2,1,0:T(8,128)(2,1)S(1)}, bf16[3,3,320,320]{3,2,1,0:T(8,128)(2,1)}, u32[]{:S(2)}) copy-start(bf16[3,3,320,320]{3,2,1,0:T(8,128)(2,1)} %param.29) | copy-start | bytes 5529604
  2.9 1.2 %copy-start.1 = (bf16[4,320,320]{2,1,0:T(8,128)(2,1)S(1)}, bf16[4,320,320]{2,1,0:T(8,128)(2,1)}, u32[]{:S(2)}) copy-start(bf16[4,320,320]{2,1,0:T(8,128)(2,1)} %refs_17_.1) | copy-start | bytes 2457604
  4.1 0.9 copy-start.2
  5.1 0.9 copy-start.3
  6.0 0.9 copy-start.4
  6.9 0.9 copy-start.5
  7.9 0.7 copy-start.6
  8.5 0.7 copy-start.7
  9.2 0.7 copy-start.8
  9.9 0.7 copy-start.9
  10.6 0.7 copy-start.10
  11.3 0.7 copy-start.11
  11.9 0.7 copy-start.12
  12.6 0.7 copy-start.13
  13.3 0.7 copy-start.14
  14.0 0.7 copy-start.15
  14.7 0.7 copy-start.16
  15.4 0.7 copy-start.17
  16.0 0.7 copy-start.18
  16.7 0.7 copy-start.19
  17.4 0.7 copy-start.20
  18.0 0.8 copy-start.21

commit v3 on v2

--- a/solution.py
+++ b/solution.py
@@ -19,7 +19,6 @@
 HD = 40
 EPS = 1e-05
 F = 16
-PIECE = 16
 PANEL_ROWS = 8 * RANK
 CHUNK = 16
 SUB = 8
@@ -49,16 +48,17 @@
     choice, degrees,
     xt, *refs,
 ):
-    vec, refs = refs[:13], refs[13:]
-    pe, k1, k2, wi, wa, wo, lower, upper, out, *refs = refs
-    xs, xh, hs, hh, act, res, proj, nown, npart, ssrc, sland, land1, src2, land2, weff, ot, *refs = refs
-    hx_s, hx_r, hh_s, hh_r, st_s, st_r, l1_s, l1_r, l2_s, l2_r, n_s, n_r = refs
-    n = nt * nr
-    pieces = PANEL_ROWS // PIECE
-    holders = min(pieces, n)
+    far, refs = refs[:19], refs[19:]
+    lower, upper, out, *refs = refs
+    near, refs = refs[:19], refs[19:]
+    vec = near[:13]
+    pe, k1, k2, wi, wa, wo = near[13:]
+    load_sem, own_sem, *refs = refs
+    xs, xh, hs, hh, act, res, proj, nown, npart, ssrc, sland, land1, src2, mid, src3, land2, weff, ot, *refs = refs
+    hx_s, hx_r, hh_s, hh_r, st_s, st_r, l1_s, l1_r, lm_s, lm_r, l2_s, l2_r, n_s, n_r = refs
+    piece = PANEL_ROWS // nr
     my_t = lax.axis_index("tm")
     my_r = lax.axis_index("rows")
-    me = my_t * nr + my_r
     side = lax.rem(my_t, 2)
     partner = my_t + 1 - 2 * side
     my_clip = my_t // 2
@@ -68,12 +68,20 @@
 
     barrier = pltpu.get_barrier_semaphore()
 
-    def greet(off, carry):
-        dst = lax.rem(me + off, n)
-        pl.semaphore_signal(barrier, inc=1, device_id=(dst // nr, lax.rem(dst, nr)), device_id_type=MESH)
-        return carry
-
-    lax.fori_loop(1, n, greet, 0)
+    def greet_row(off, carry):
+        pl.semaphore_signal(barrier, inc=1, device_id=(my_t, lax.rem(my_r + off, nr)), device_id_type=MESH)
+        return carry
+
+    def greet_column(off, carry):
+        pl.semaphore_signal(barrier, inc=1, device_id=(lax.rem(my_t + off, nt), my_r), device_id_type=MESH)
+        return carry
+
+    lax.fori_loop(1, nr, greet_row, 0)
+    lax.fori_loop(1, nt, greet_column, 0)
+
+    loads = [pltpu.make_async_copy(a, b, load_sem.at[i]) for i, (a, b) in enumerate(zip(far, near))]
+    for i in (*range(13), 14, 15, 13, 16, 17, 18):
+        loads[i].start()
 
     row = lambda i: vec[i][...].reshape(1, C)
     gc = lax.broadcasted_iota(jnp.int32, (C, 128), 0)
@@ -210,45 +218,52 @@
     for r in range(strip + 2):
         act[r, 0] = jnp.zeros((F, C), BF16)
         act[r, W + 1] = jnp.zeros((F, C), BF16)
-    pl.semaphore_wait(barrier, n - 1)
+    pl.semaphore_wait(barrier, nr + nt - 2)
     send_stats(0)
     send_halo(xs, xh, hx_s, hx_r)
 
-    half = pieces // 2
+    half = nr // 2
 
     def rows_of(p):
-        return pl.ds(pl.multiple_of(p * PIECE, PIECE), PIECE)
+        return pl.ds(pl.multiple_of(p * piece, piece), piece)
 
     def piece_copy(p, panel, first):
         return pltpu.make_async_remote_copy(
-            src_ref=panel.at[rows_of(p - first)], dst_ref=land1.at[me],
-            send_sem=l1_s.at[p], recv_sem=l1_r.at[me],
-            device_id=(p // nr, lax.rem(p, nr)), device_id_type=MESH)
+            src_ref=panel.at[rows_of(p - first)], dst_ref=land1.at[my_r],
+            send_sem=l1_s.at[p], recv_sem=l1_r.at[my_r],
+            device_id=(my_t, p), device_id_type=MESH)
 
     def piece_start(off, carry):
-        p = lax.rem(me + off, n)
+        p = lax.rem(my_r + off, nr)
 
         @pl.when(p < half)
         def _():
             piece_copy(p, lower, 0).start()
 
-        @pl.when((p >= half) & (p < holders))
+        @pl.when(p >= half)
         def _():
             piece_copy(p, upper, half).start()
         return carry
 
-    lax.fori_loop(1, n, piece_start, 0)
-
-    @pl.when(me < half)
+    lax.fori_loop(1, nr, piece_start, 0)
+
+    def own_piece(panel, first):
+        return pltpu.make_async_copy(panel.at[rows_of(my_r - first)], land1.at[my_r], own_sem.at[0])
+
+    @pl.when(my_r < half)
     def _():
-        land1[me] = lower[rows_of(me)]
-
-    @pl.when((me >= half) & (me < holders))
+        own_piece(lower, 0).start()
+
+    @pl.when(my_r >= half)
     def _():
-        land1[me] = upper[rows_of(me - half)]
-
+        own_piece(upper, half).start()
+
+    for i in range(13):
+        loads[i].wait()
     scale, shift = get_stats(0, row(0), row(1))
     activate(xs, xh, hx_s, hx_r, scale, shift)
+
+    loads[14].wait()
 
     def conv_one(r, carry):
         total, square = carry
@@ -262,35 +277,57 @@
     put_stats(1, total, square)
     send_stats(1)
 
-    def share_copy(dst):
-        return pltpu.make_async_remote_copy(
-            src_ref=src2.at[(dst // nr) // 2], dst_ref=land2.at[me],
-            send_sem=l2_s.at[dst], recv_sem=l2_r.at[me],
-            device_id=(dst // nr, lax.rem(dst, nr)), device_id_type=MESH)
-
-    @pl.when(me < holders)
-    def _():
-        def piece_wait(off, carry):
-            s = lax.rem(me + off, n)
-            pltpu.make_async_remote_copy(
-                src_ref=lower.at[pl.ds(0, PIECE)], dst_ref=land1.at[s],
-                send_sem=l1_s.at[0], recv_sem=l1_r.at[s],
-                device_id=(s // nr, lax.rem(s, nr)), device_id_type=MESH).wait_recv()
-            return carry
-
-        lax.fori_loop(1, n, piece_wait, 0)
-        for k in range(clips):
-            src2[k] = land1[choice[k]]
-        land2[me] = src2[my_clip]
-
-        def share(off, carry):
-            share_copy(lax.rem(me + off, n)).start()
-            return carry
-
-        lax.fori_loop(1, n, share, 0)
+    def pass_copy(t):
+        return pltpu.make_async_remote_copy(
+            src_ref=src2.at[t // 2], dst_ref=mid.at[my_t], send_sem=lm_s.at[t], recv_sem=lm_r.at[my_t],
+            device_id=(t, my_r), device_id_type=MESH)
+
+    def piece_wait(off, carry):
+        p = lax.rem(my_r + off, nr)
+        pltpu.make_async_remote_copy(
+            src_ref=lower.at[pl.ds(0, piece)], dst_ref=land1.at[p],
+            send_sem=l1_s.at[p], recv_sem=l1_r.at[p],
+            device_id=(my_t, p), device_id_type=MESH).wait_recv()
+        return carry
+
+    lax.fori_loop(1, nr, piece_wait, 0)
+    own_piece(lower, my_r).wait()
+    for k in range(clips):
+        src2[k] = land1[lax.rem(choice[k], nr)]
+    mid[my_t] = src2[my_clip]
+
+    def pass_start(off, carry):
+        pass_copy(lax.rem(my_t + off, nt)).start()
+        return carry
+
+    lax.fori_loop(1, nt, pass_start, 0)
 
     scale, shift = get_stats(1, row(3), row(4))
     activate(hs, hh, hh_s, hh_r, scale, shift)
+
+    def share_copy(p):
+        return pltpu.make_async_remote_copy(
+            src_ref=src3, dst_ref=land2.at[my_r], send_sem=l2_s.at[p], recv_sem=l2_r.at[my_r],
+            device_id=(my_t, p), device_id_type=MESH)
+
+    def pass_wait(off, carry):
+        t = lax.rem(my_t + off, nt)
+        pltpu.make_async_remote_copy(
+            src_ref=src2.at[0], dst_ref=mid.at[t], send_sem=lm_s.at[t], recv_sem=lm_r.at[t],
+            device_id=(t, my_r), device_id_type=MESH).wait_recv()
+        return carry
+
+    lax.fori_loop(1, nt, pass_wait, 0)
+    chosen = mid[choice[my_clip] // nr]
+    src3[...] = chosen
+    land2[my_r] = chosen
+
+    def share_start(off, carry):
+        share_copy(lax.rem(my_r + off, nr)).start()
+        return carry
+
+    lax.fori_loop(1, nr, share_start, 0)
+    loads[15].wait()
 
     def conv_two(r, carry):
         total, square = carry
@@ -305,20 +342,18 @@
     send_stats(2)
 
     def share_wait(off, carry):
-        s = lax.rem(me + off, n)
-
-        @pl.when(s < holders)
-        def _():
-            pltpu.make_async_remote_copy(
-                src_ref=src2.at[0], dst_ref=land2.at[s],
-                send_sem=l2_s.at[0], recv_sem=l2_r.at[s],
-                device_id=(s // nr, lax.rem(s, nr)), device_id_type=MESH).wait_recv()
-        return carry
-
-    lax.fori_loop(1, n, share_wait, 0)
+        p = lax.rem(my_r + off, nr)
+        pltpu.make_async_remote_copy(
+            src_ref=src3, dst_ref=land2.at[p], send_sem=l2_s.at[p], recv_sem=l2_r.at[p],
+            device_id=(my_t, p), device_id_type=MESH).wait_recv()
+        return carry
+
+    lax.fori_loop(1, nr, share_wait, 0)
+    for i in (13, 16, 17, 18):
+        loads[i].wait()
     degree = degrees[my_clip]
     kept = lax.broadcasted_iota(jnp.int32, (RANK, C), 0) < degree
-    per = RANK // PIECE
+    per = RANK // piece
     for j in range(4):
         down = land2[j * per : (j + 1) * per].reshape(RANK, C)
         down = jnp.where(kept, down.astype(F32), 0.0).astype(BF16)
@@ -404,22 +439,17 @@
     halo_sent(hs, hh, hh_s, hh_r)
 
     def piece_sent(off, carry):
-        p = lax.rem(me + off, n)
-
-        @pl.when(p < holders)
-        def _():
-            piece_copy(p, lower, p).wait_send()
-        return carry
-
-    lax.fori_loop(1, n, piece_sent, 0)
-
-    @pl.when(me < holders)
-    def _():
-        def share_sent(off, carry):
-            share_copy(lax.rem(me + off, n)).wait_send()
-            return carry
-
-        lax.fori_loop(1, n, share_sent, 0)
+        p = lax.rem(my_r + off, nr)
+        piece_copy(p, lower, p).wait_send()
+        share_copy(p).wait_send()
+        return carry
+
+    def pass_sent(off, carry):
+        pass_copy(lax.rem(my_t + off, nt)).wait_send()
+        return carry
+
+    lax.fori_loop(1, nr, piece_sent, 0)
+    lax.fori_loop(1, nt, pass_sent, 0)
 
 
 def per_device(
@@ -428,7 +458,6 @@
     wi, bi, ln_gain, ln_shift, wa, ab, lower, raise_, wo, ob,
 ):
     nt, nr = lax.axis_size("tm"), lax.axis_size("rows")
-    n = nt * nr
     strip = latents.shape[1]
     clips = choice.shape[0]
     xt = jnp.transpose(latents, (1, 0, 2))
@@ -438,14 +467,16 @@
     vmem = pl.BlockSpec(memory_space=pltpu.VMEM)
     smem = pl.BlockSpec(memory_space=pltpu.SMEM)
     chunks = strip * W // CHUNK
-    holders = min(PANEL_ROWS // PIECE, n)
+    piece = PANEL_ROWS // nr
     dma = pltpu.SemaphoreType.DMA
+    params = [*vec, jnp.asarray(positions()), k1.reshape(9, C, C), k2.reshape(9, C, C), wi, wa, wo]
     out = pl.pallas_call(
         functools.partial(kernel, nt, nr, strip, clips),
         out_shape=jax.ShapeDtypeStruct(xt.shape, BF16),
-        in_specs=[smem, smem] + [vmem] * 22,
+        in_specs=[smem, smem, vmem] + [pl.BlockSpec(memory_space=pltpu.HBM)] * 21,
         out_specs=vmem,
-        scratch_shapes=[
+        scratch_shapes=[pltpu.VMEM(a.shape, a.dtype) for a in params] + [
+            dma((len(params),)), dma((1,)),
             pltpu.VMEM((strip, W, F, C), BF16),
             pltpu.VMEM((2, W, F, C), BF16),
             pltpu.VMEM((strip, W, F, C), BF16),
@@ -457,22 +488,23 @@
             pltpu.VMEM((chunks, CHUNK * F, C), BF16),
             pltpu.VMEM((3, F, 128), F32),
             pltpu.VMEM((3, nr, F, 128), F32),
-            pltpu.VMEM((n, PIECE, C), BF16),
-            pltpu.VMEM((clips, PIECE, C), BF16),
-            pltpu.VMEM((holders, PIECE, C), BF16),
+            pltpu.VMEM((nr, piece, C), BF16),
+            pltpu.VMEM((clips, piece, C), BF16),
+            pltpu.VMEM((nt, piece, C), BF16),
+            pltpu.VMEM((piece, C), BF16),
+            pltpu.VMEM((nr, piece, C), BF16),
             pltpu.VMEM((4, C, C), BF16),
             pltpu.VMEM((C, CHUNK * F), F32),
             dma((2,)), dma((2,)), dma((2,)), dma((2,)),
             dma((3, nr)), dma((3, nr)),
-            dma((holders,)), dma((n,)), dma((n,)), dma((holders,)),
+            dma((nr,)), dma((nr,)), dma((nt,)), dma((nt,)), dma((nr,)), dma((nr,)),
             dma((chunks,)), dma((chunks,)),
         ],
         compiler_params=pltpu.CompilerParams(
-            collective_id=0, has_side_effects=True, vmem_limit_bytes=48 * 1024 * 1024),
+            collective_id=0, has_side_effects=True, vmem_limit_bytes=64 * 1024 * 1024),
         cost_estimate=pl.CostEstimate(flops=6 * 10**9, bytes_accessed=8 * 10**6, transcendentals=3 * 10**6),
     )(
-        choice, degrees, xt, *vec, jnp.asarray(positions()),
-        k1.reshape(9, C, C), k2.reshape(9, C, C), wi, wa, wo, lower, upper)
+        choice, degrees, xt, *params, lower, upper)
     return jnp.transpose(out, (1, 0, 2))
 
 

time: 103 us -> 83.2 us (0.81)
  local copies, waits for them, and re-layouts: 20.3 us -> 4.71 us
  Pallas kernels: 82.2 us -> 78.2 us
    unnamed x45 -> x1, local copies, waits for them, and re-layouts: 18.8 us -> 2.12 us
    pallas_call x1, Pallas kernels: 82.2 us -> 78.2 us  [per_device(): pl.pallas_call(functools.partial(kernel, nt, nr, strip, clips), out_shape...]
    transpose x1, local copies, waits for them, and re-layouts: 1.51 us -> 2.6 us  [per_device(): return jnp.transpose(out, (1, 0, 2))]
where the time goes in v3:
time: 83.2 us; the launch traced here: 83 us
  Pallas kernels  78.2 us (94%)
  local copies, waits for them, and re-layouts  4.71 us (6%)
    pallas_call x1, Pallas kernels, per_device(): pl.pallas_call(functools.partial(kernel, nt, nr, strip, clips), out_shape...  78.2 us
    transpose x1, local copies, waits for them, and re-layouts, per_device(): return jnp.transpose(out, (1, 0, 2))  2.6 us
    unnamed x1, local copies, waits for them, and re-layouts  2.12 us

profile of v3, /device:TPU:0, one launch (start us, length us, event | category | flops | bytes accessed | tf_op | source)
XLA Modules:
  0.0 83.0 jit_solution(11755535339907368392)
XLA Ops:
  0.0 2.1 %copy.28 = bf16[16,2,10240]{2,0,1:T(8,128)(2,1)} copy(bf16[16,2,10240]{2,1,0:T(2,128)(2,1)} %param.24) | data formatting | bytes 1310720 | tf_op args[0]
  2.1 78.2 %shard_map.226 = bf16[2,16,10240]{2,1,0:T(8,128)(2,1)} custom-call(s32[2]{0:T(128)} %choice.1, s32[2]{0:T(128)} %degrees.1, bf16[2,16,10240]{2,1,0:T(8,128)(2,1)} %bitcast.13, f32[320]{0:T(512)} %refs_0_.1, f32[320]{0:T(512)} %refs_1_.1, f32[320]{0:T(512)} %refs_2_.1, f32[320]{0:T(512)} %refs_3_.1, f32[320]{0:T(512)} %refs_4_.1, f32[320]{0:T(512)} %refs_5_.1, ...), custom_call_target="tpu_custom_call" | custom-call | flops 6000000000 | bytes 8000000 | tf_op jit(solution)/shard_map/pallas_call | solution.py:473
  80.4 2.6 %copy.26 = bf16[16,2,10240]{2,1,0:T(2,128)(2,1)} copy(bf16[16,2,10240]{2,0,1:T(8,128)(2,1)} %bitcast.12) | data formatting | bytes 1310720 | tf_op jit(solution)/shard_map/transpose | solution.py:508

commit v4 on v3

--- a/solution.py
+++ b/solution.py
@@ -127,13 +127,13 @@
         def step(off, carry):
             stat_copy(i, off).start()
             return carry
-        lax.fori_loop(1, nr, step, 0)
+        lax.fori_loop(1, nr, step, 0, unroll=True)
 
     def get_stats(i, gain, shift):
         def step(off, carry):
             stat_wait(i, off).wait_recv()
             return carry
-        lax.fori_loop(1, nr, step, 0)
+        lax.fori_loop(1, nr, step, 0, unroll=True)
         total = sland[i, 0]
         for s in range(1, nr):
             total = total + sland[i, s]
@@ -213,7 +213,7 @@
                 total = term if total is None else total + term
         return total
 
-    total, square = lax.fori_loop(0, W // 2, unpack, (zero, zero))
+    total, square = lax.fori_loop(0, W // 2, unpack, (zero, zero), unroll=2)
     put_stats(0, total, square)
     for r in range(strip + 2):
         act[r, 0] = jnp.zeros((F, C), BF16)
@@ -385,7 +385,7 @@
         chunk_copy(c).start()
         return carry
 
-    lax.fori_loop(0, chunks, project, 0)
+    lax.fori_loop(0, chunks, project, 0, unroll=2)
 
     rows = SUB * F
     key_pixel = lax.rem(lax.broadcasted_iota(jnp.int32, (2 * rows, rows), 0), rows) // F
@@ -434,7 +434,7 @@
         def step(off, carry):
             stat_copy(i, off).wait_send()
             return carry
-        lax.fori_loop(1, nr, step, 0)
+        lax.fori_loop(1, nr, step, 0, unroll=True)
     halo_sent(xs, xh, hx_s, hx_r)
     halo_sent(hs, hh, hh_s, hh_r)
 

time: 83.2 us -> 82.4 us (level)
  no operation moved by 1% of the time
where the time goes in v4:
time: 82.4 us; the launch traced here: 82.1 us
  Pallas kernels  77.4 us (94%)
  local copies, waits for them, and re-layouts  4.71 us (6%)
    pallas_call x1, Pallas kernels, per_device(): pl.pallas_call(functools.partial(kernel, nt, nr, strip, clips), out_shape...  77.4 us
    transpose x1, local copies, waits for them, and re-layouts, per_device(): return jnp.transpose(out, (1, 0, 2))  2.6 us
    unnamed x1, local copies, waits for them, and re-layouts  2.12 us

profile of v4, /device:TPU:0, one launch (start us, length us, event | category | flops | bytes accessed | tf_op | source)
XLA Modules:
  0.0 82.1 jit_solution(9364762263038199133)
XLA Ops:
  0.0 2.1 %copy.28 = bf16[16,2,10240]{2,0,1:T(8,128)(2,1)} copy(bf16[16,2,10240]{2,1,0:T(2,128)(2,1)} %param.24) | data formatting | bytes 1310720 | tf_op args[0]
  2.1 77.4 %shard_map.226 = bf16[2,16,10240]{2,1,0:T(8,128)(2,1)} custom-call(s32[2]{0:T(128)} %choice.1, s32[2]{0:T(128)} %degrees.1, bf16[2,16,10240]{2,1,0:T(8,128)(2,1)} %bitcast.13, f32[320]{0:T(512)} %refs_0_.1, f32[320]{0:T(512)} %refs_1_.1, f32[320]{0:T(512)} %refs_2_.1, f32[320]{0:T(512)} %refs_3_.1, f32[320]{0:T(512)} %refs_4_.1, f32[320]{0:T(512)} %refs_5_.1, ...), custom_call_target="tpu_custom_call" | custom-call | flops 6000000000 | bytes 8000000 | tf_op jit(solution)/shard_map/pallas_call | solution.py:473
  79.5 2.6 %copy.26 = bf16[16,2,10240]{2,1,0:T(2,128)(2,1)} copy(bf16[16,2,10240]{2,0,1:T(8,128)(2,1)} %bitcast.12) | data formatting | bytes 1310720 | tf_op jit(solution)/shard_map/transpose | solution.py:508
